TPU v7x, 768 devices: a whole 4x8x12 slice. The times are simulated.
768 devices in a mesh: dom: 16 (over x, z_lo), grp: 48 (over z_hi, y, core).
Axes of the slice: x: 4, y: 8, z: 12 (z_hi: 3, z_lo: 4; z = z_hi * 4 + z_lo), core: 2. Of those that a mesh axis runs over, the one named last changes fastest.
Arguments:
- features: float32 [196608, 768], P(('dom', 'grp')), may hold values from -6 to 6
- factor: float32 [768, 768], P(None, 'grp'), as said below
- slab_map: int32 [196608], P('dom'), may hold values from 0 to 12287, as said below
- kinds: int32 [192, 8, 128], P('dom'), may hold values from 0 to 7
- kind_table: float32 [8, 27], replicated, may hold values from -0.15 to 0.15
Outputs:
- filtered: float32 [768, 192, 8, 128], P('grp', 'dom')
Inputs may be any that keep to these rules, and one draw needn't show every extreme that they name: `slab_map`: each aligned block of 12288 entries (one slab) is a permutation of 0 to 12287. `factor`: upper triangular with diagonal between 0.5 and 1.5.
All inputs are finite; a program needn't handle non-finite values.
Results may differ from a plain program's by a relative error of at most 0.00009.
Values sent between devices are 32-bit elements; how exact they have to be, the bound alone decides.
A program may use at most 64 MiB of HBM per device.

v0:
```python
import jax
import jax.numpy as jnp
from jax import lax
from jax.sharding import PartitionSpec as P

CHEB = 4


def padded_2(cells, sides, width):
    for axis, dim in sides:
        count = lax.axis_size(axis)
        ends = count - 1
        head = lax.slice_in_dim(cells, 0, width, axis=dim)
        tail = lax.slice_in_dim(cells, cells.shape[dim] - width, cells.shape[dim], axis=dim)
        cells = jnp.concatenate(
            [
                lax.ppermute(tail, axis, [(i, (i + 1) % count) for i in range(ends)]),
                cells,
                lax.ppermute(head, axis, [((i + 1) % count, i) for i in range(ends)]),
            ],
            axis=dim,
        )
    return cells


def stencil_apply(values, coeffs):
    planes = values.shape[1] - 2
    extent_y = values.shape[2]
    extent_z = values.shape[3]
    padded = jnp.pad(values, ((0, 0), (0, 0), (1, 1), (1, 1)))
    summed = jnp.zeros((values.shape[0], planes, extent_y, extent_z), jnp.float32)
    for shift_x in (-1, 0, 1):
        for shift_y in (-1, 0, 1):
            for shift_z in (-1, 0, 1):
                offset = (shift_x + 1) * 9 + (shift_y + 1) * 3 + (shift_z + 1)
                window = padded[
                    :,
                    1 + shift_x : 1 + shift_x + planes,
                    1 + shift_y : 1 + shift_y + extent_y,
                    1 + shift_z : 1 + shift_z + extent_z,
                ]
                summed = summed + coeffs[offset][None] * window
    return summed


def local(features, factor, slab_map, kinds, kind_table):
    numbers = (((0,), (1,)), ((), ()))
    columns = lax.all_gather(factor, "grp", axis=1, tiled=True)
    rotated = lax.dot_general(
        columns,
        features,
        numbers,
        precision=lax.Precision.HIGHEST,
        preferred_element_type=jnp.float32,
    )
    moved = lax.all_to_all(rotated, "grp", split_axis=0, concat_axis=1, tiled=True)
    states_here = moved.shape[0]
    lattice = jnp.zeros_like(moved).at[:, slab_map].set(moved)
    lattice = lattice.reshape(states_here, -1, kinds.shape[1], kinds.shape[2])
    thickness = lattice.shape[1]
    wider_kinds = padded_2(kinds, (("dom", 0),), 1)
    onehot = (
        wider_kinds[None] == jnp.arange(kind_table.shape[0], dtype=jnp.int32)[:, None, None, None]
    ).astype(jnp.float32)
    coeffs = jnp.einsum("ko,kxyz->oxyz", kind_table, onehot, precision=lax.Precision.HIGHEST)
    position = lax.axis_index("dom") * thickness + jnp.arange(thickness + 2, dtype=jnp.int32) - 1
    inside = ((position >= 0) & (position < thickness * lax.axis_size("dom"))).astype(jnp.float32)[
        None, :, None, None
    ]
    earlier = jnp.zeros_like(lattice)
    current = lattice
    for paired in range(CHEB // 2):
        stacked = padded_2(jnp.stack([earlier, current]), (("dom", 2),), 2)
        wide_earlier = stacked[0]
        wide_current = stacked[1]
        if paired == 0:
            middle = stencil_apply(wide_current, coeffs)
        else:
            middle = 2.0 * stencil_apply(wide_current, coeffs) - wide_earlier[:, 1:-1]
        middle = middle * inside
        following = 2.0 * stencil_apply(middle, coeffs[:, 1:-1]) - wide_current[:, 2:-2]
        earlier = middle[:, 1:-1]
        current = following
    return current


def solution(mesh):
    return jax.shard_map(
        local,
        mesh=mesh,
        in_specs=(P(("dom", "grp"), None), P(None, "grp"), P("dom"), P("dom", None, None), P()),
        out_specs=P("grp", "dom", None, None),
        check_vma=False,
    )
```

profile of v0, /device:TPU:6, one launch (start us, length us, event | category | flops | bytes accessed | tf_op | source)
XLA Modules:
  0.0 272.3 jit_solution(15568951669909378265)
XLA Ops:
  6.5 0.7 all-gather.2.cloned.1.call-update
  7.3 115.6 %all-gather.2.cloned.1.call-done = f32[768,768]{0,1:T(8,128)} async-done(((f32[768,16]{0,1:T(8,128)}), f32[768,768]{0,1:T(8,128)}) %all-gather.2.cloned.1.call-update) | async-done | bytes 2359312 | tf_op jit(solution)/shard_map/all_gather | solution.py:48
  122.9 4.6 %fusion.219 = f32[768,256]{1,0:T(8,128)} fusion(f32[768,768]{0,1:T(8,128)} %all-gather.2.cloned.1.call-done, f32[256,768]{1,0:T(8,128)S(1)} %copy-done), kind=kOutput, calls=%fused_computation.342 | convolution fusion | flops 1811939328 | bytes 3932160 | tf_op jit(solution)/shard_map/dot_general | solution.py:49
  127.5 9.3 %all-to-all-start = ((f32[48,16,256]{2,1,0:T(8,128)}), f32[48,16,256]{2,1,0:T(8,128)S(1)}, u32[]{:S(2)}, u32[]{:S(2)}) async-start(f32[48,16,256]{2,1,0:T(8,128)} %bitcast.5), calls=%async_computation | async-start | bytes 1572864 | tf_op jit(solution)/shard_map/all_to_all | solution.py:56
  136.8 3.9 %collective-permute-start.1 = (s32[1,8,128]{2,1,0:T(8,128)S(1)}, s32[1,8,128]{2,1,0:T(8,128)S(1)}, u32[]{:S(2)}, u32[]{:S(2)}) collective-permute-start(s32[1,8,128]{2,1,0:T(8,128)S(1)} %get-tuple-element.66), channel_id=1, source_target_pairs={{48,0},{96,48},{144,96},{192,144},{240,192},{288,240},{336,288},{3... | collective-permute-start | bytes 12296 | tf_op jit(solution)/shard_map/ppermute | solution.py:19
  140.7 1.9 collective-permute-start
  142.7 0.6 compare_select_fusion
  143.3 19.9 %collective-permute-done.1 = s32[1,8,128]{2,1,0:T(8,128)S(1)} collective-permute-done((s32[1,8,128]{2,1,0:T(8,128)S(1)}, s32[1,8,128]{2,1,0:T(8,128)S(1)}, u32[]{:S(2)}, u32[]{:S(2)}) %collective-permute-start.1) | collective-permute-done | bytes 4128 | tf_op jit(solution)/shard_map/ppermute | solution.py:19
  163.2 0.9 convolution_bitcast_fusion
  164.2 1.5 fusion.214
  165.7 1.7 fusion.216
  167.4 4.8 %all-to-all-done = f32[48,16,256]{2,1,0:T(8,128)S(1)} async-done(((f32[48,16,256]{2,1,0:T(8,128)}), f32[48,16,256]{2,1,0:T(8,128)S(1)}, u32[]{:S(2)}, u32[]{:S(2)}) %all-to-all-start) | async-done | bytes 786464 | tf_op jit(solution)/shard_map/all_to_all | solution.py:56
  172.2 4.0 %copy.6 = f32[16,48,256]{0,2,1:T(8,128)} copy(f32[16,48,256]{2,0,1:T(8,128)S(1)} %bitcast.81) | data formatting | bytes 1572864 | tf_op jit(solution)/shard_map/all_to_all | solution.py:56
  176.1 33.8 %scatter_custom_fusion = f32[16,12288]{0,1:T(8,128)} fusion(s32[12288]{0:T(1024)} %compare_select_fusion, f32[12288,16]{1,0:T(8,128)} %bitcast.80, f32[]{:T(128)} %constant.9.clone.1), kind=kCustom, calls=%fused_computation.97 | custom fusion | bytes 786944 | tf_op jit(solution)/shard_map/scatter | solution.py:58
  210.0 4.4 %copy.7 = f32[1,16,12,8,128]{4,3,2,1,0:T(8,128)S(1)} copy(f32[1,16,12,8,128]{1,4,3,2,0:T(8,128)} %bitcast.79) | data formatting | bytes 1572864 | tf_op jit(solution)/shard_map/stack;reshape | solution.py:73
  214.4 2.2 collective-permute-start.3
  216.7 3.8 %collective-permute-start.2 = (f32[2,16,2,8,128]{4,3,2,1,0:T(8,128)S(1)}, f32[2,16,2,8,128]{4,3,2,1,0:T(8,128)S(1)}, u32[]{:S(2)}, u32[]{:S(2)}) collective-permute-start(f32[2,16,2,8,128]{4,3,2,1,0:T(8,128)S(1)} %get-tuple-element.63), channel_id=1, source_target_pairs={{0,48},{48,96},{96,144},{144,192},{192,240},{240,288},{288,336},{3... | collective-permute-start | bytes 786440 | tf_op jit(solution)/shard_map/ppermute | solution.py:17
  220.5 0.3 fusion.215
  220.8 0.3 fusion.217
  221.1 0.2 stack.12
  221.4 3.2 %collective-permute-done.3 = f32[2,16,2,8,128]{4,3,2,1,0:T(8,128)S(1)} collective-permute-done((f32[2,16,2,8,128]{4,3,2,1,0:T(8,128)S(1)}, f32[2,16,2,8,128]{4,3,2,1,0:T(8,128)S(1)}, u32[]{:S(2)}, u32[]{:S(2)}) %collective-permute-start.3) | collective-permute-done | bytes 262176 | tf_op jit(solution)/shard_map/ppermute | solution.py:19
  224.6 4.7 %collective-permute-done.2 = f32[2,16,2,8,128]{4,3,2,1,0:T(8,128)S(1)} collective-permute-done((f32[2,16,2,8,128]{4,3,2,1,0:T(8,128)S(1)}, f32[2,16,2,8,128]{4,3,2,1,0:T(8,128)S(1)}, u32[]{:S(2)}, u32[]{:S(2)}) %collective-permute-start.2) | collective-permute-done | bytes 262176 | tf_op jit(solution)/shard_map/ppermute | solution.py:17
  229.8 4.5 %fusion.48 = f32[16,14,8,128]{3,2,1,0:T(8,128)S(1)} fusion(f32[16,16,8,128]{3,2,1,0:T(8,128)S(1)} %fusion.2, f32[14]{0:T(128)S(1)} %and_convert_fusion, f32[14,8,128]{2,1,0:T(8,128)S(1)} %bitcast.100, f32[14,8,128]{2,1,0:T(8,128)S(1)} %bitcast.102, f32[14,8,128]{2,1,0:T(8,128)S(1)} %bitcast.104, f32[14,8,128]{2,1,0:T(8,128)S(1)} %bitcast.106, ...), kind=kLoop, calls=%fused_computation.151 | loop fusion | flops 12386304 | bytes 6267392 | tf_op jit(solution)/shard_map/mul | solution.py:80
  234.6 3.9 %fusion.154 = f32[1,16,12,8,128]{4,3,2,1,0:T(8,128)S(1)} fusion(f32[16,14,8,128]{3,2,1,0:T(8,128)S(1)} %fusion.48, f32[16,16,8,128]{3,2,1,0:T(8,128)S(1)} %fusion.2, f32[12,8,128]{2,1,0:T(8,128)S(1)} %bitcast.154, f32[12,8,128]{2,1,0:T(8,128)S(1)} %bitcast.156, f32[12,8,128]{2,1,0:T(8,128)S(1)} %bitcast.158, f32[12,8,128]{2,1,0:T(8,128)S(1)} %bitcast.160, ...), kind=kLoop, calls=%fused_computation.263 | loop fusion | flops 10813440 | bytes 6176768 | tf_op jit(solution)/shard_map/stack | solution.py:73
  238.5 4.7 %collective-permute-start.5 = (f32[2,16,2,8,128]{4,3,2,1,0:T(8,128)S(1)}, f32[2,16,2,8,128]{4,3,2,1,0:T(8,128)S(1)}, u32[]{:S(2)}, u32[]{:S(2)}) collective-permute-start(f32[2,16,2,8,128]{4,3,2,1,0:T(8,128)S(1)} %get-tuple-element.62), channel_id=1, source_target_pairs={{48,0},{96,48},{144,96},{192,144},{240,192},{288,240},{336,288},{3... | collective-permute-start | bytes 786440 | tf_op jit(solution)/shard_map/ppermute | solution.py:19
  243.3 1.9 collective-permute-start.4
  245.2 4.8 %collective-permute-done.5 = f32[2,16,2,8,128]{4,3,2,1,0:T(8,128)S(1)} collective-permute-done((f32[2,16,2,8,128]{4,3,2,1,0:T(8,128)S(1)}, f32[2,16,2,8,128]{4,3,2,1,0:T(8,128)S(1)}, u32[]{:S(2)}, u32[]{:S(2)}) %collective-permute-start.5) | collective-permute-done | bytes 262176 | tf_op jit(solution)/shard_map/ppermute | solution.py:19
  250.0 6.0 %collective-permute-done.4 = f32[2,16,2,8,128]{4,3,2,1,0:T(8,128)S(1)} collective-permute-done((f32[2,16,2,8,128]{4,3,2,1,0:T(8,128)S(1)}, f32[2,16,2,8,128]{4,3,2,1,0:T(8,128)S(1)}, u32[]{:S(2)}, u32[]{:S(2)}) %collective-permute-start.4) | collective-permute-done | bytes 262176 | tf_op jit(solution)/shard_map/ppermute | solution.py:17
  256.0 0.2 pad_maximum_fusion
  256.1 0.1 slice_bitcast_fusion
  256.3 4.5 %fusion.101 = f32[16,14,8,128]{3,2,1,0:T(8,128)S(1)} fusion(f32[16,16,8,128]{3,2,1,0:T(8,128)S(1)} %get-tuple-element.6, f32[16,16,8,128]{3,2,1,0:T(8,128)S(1)} %get-tuple-element.5, f32[14]{0:T(128)S(1)} %and_convert_fusion, f32[14,8,128]{2,1,0:T(8,128)S(1)} %bitcast.101, f32[14,8,128]{2,1,0:T(8,128)S(1)} %bitcast.103, f32[14,8,128]{2,1,0:T(8,128)S(1)} %bitcast.105, ...), kind=kLoop, calls=%fused_computation.204 | loop fusion | flops 12845056 | bytes 7184896 | tf_op jit(solution)/shard_map/mul | solution.py:80
  260.8 4.6 %fusion.206 = f32[16,12,8,128]{3,2,1,0:T(8,128)} fusion(f32[16,14,8,128]{3,2,1,0:T(8,128)S(1)} %fusion.101, f32[16,16,8,128]{3,2,1,0:T(8,128)S(1)} %get-tuple-element.6, f32[12,8,128]{2,1,0:T(8,128)S(1)} %bitcast.155, f32[12,8,128]{2,1,0:T(8,128)S(1)} %bitcast.157, f32[12,8,128]{2,1,0:T(8,128)S(1)} %bitcast.159, f32[12,8,128]{2,1,0:T(8,128)S(1)} %bitcast.161, ...), kind=kLoop, calls=%fused_computation.315 | loop fusion | flops 10813440 | bytes 6176768 | tf_op jit(solution)/shard_map/sub | solution.py:81
  (89 shorter events, 0.4 us)
Async XLA Ops:
  6.5 116.4 %copy-start = (f32[256,768]{1,0:T(8,128)S(1)}, f32[256,768]{1,0:T(8,128)}, u32[]{:S(2)}) copy-start(f32[256,768]{1,0:T(8,128)} %param.5) | copy-start | bytes 2359300
  6.5 116.4 %all-gather.2.cloned.1.call-start = ((), (), s32[]{:S(2)}) async-start(), calls=%async_computation.1 | async-start | bytes 2408448 | tf_op jit(solution)/shard_map/all_gather | solution.py:48
  7.3 129.5 %copy-start.37 = (s32[12,8,128]{2,1,0:T(8,128)S(1)}, s32[12,8,128]{2,1,0:T(8,128)}, u32[]{:S(2)}) copy-start(s32[12,8,128]{2,1,0:T(8,128)} %param.8) | copy-start | bytes 147460
  7.3 135.4 %copy-start.38 = (s32[12288]{0:T(1024)S(1)}, s32[12288]{0:T(1024)}, u32[]{:S(2)}) copy-start(s32[12288]{0:T(1024)} %param.7) | copy-start | bytes 147460
  7.3 156.0 %copy-start.39 = (f32[8,27]{1,0:T(8,128)S(1)}, f32[8,27]{1,0:T(8,128)}, u32[]{:S(2)}) copy-start(f32[8,27]{1,0:T(8,128)} %param.9) | copy-start | bytes 2596
  127.5 44.7 %all-to-all-start = ((f32[48,16,256]{2,1,0:T(8,128)}), f32[48,16,256]{2,1,0:T(8,128)S(1)}, u32[]{:S(2)}, u32[]{:S(2)}) async-start(f32[48,16,256]{2,1,0:T(8,128)} %bitcast.5), calls=%async_computation | async-start | bytes 1572864 | tf_op jit(solution)/shard_map/all_to_all | solution.py:56
  136.8 26.4 %collective-permute-start.1 = (s32[1,8,128]{2,1,0:T(8,128)S(1)}, s32[1,8,128]{2,1,0:T(8,128)S(1)}, u32[]{:S(2)}, u32[]{:S(2)}) collective-permute-start(s32[1,8,128]{2,1,0:T(8,128)S(1)} %get-tuple-element.66), channel_id=1, source_target_pairs={{48,0},{96,48},{144,96},{192,144},{240,192},{288,240},{336,288},{3... | collective-permute-start | bytes 12296 | tf_op jit(solution)/shard_map/ppermute | solution.py:19
  140.7 22.5 %collective-permute-start = (s32[1,8,128]{2,1,0:T(8,128)S(1)}, s32[1,8,128]{2,1,0:T(8,128)S(1)}, u32[]{:S(2)}, u32[]{:S(2)}) collective-permute-start(s32[1,8,128]{2,1,0:T(8,128)S(1)} %get-tuple-element.65), channel_id=1, source_target_pairs={{0,48},{48,96},{96,144},{144,192},{192,240},{240,288},{288,336},{3... | collective-permute-start | bytes 12296 | tf_op jit(solution)/shard_map/ppermute | solution.py:17
  214.4 10.2 %collective-permute-start.3 = (f32[2,16,2,8,128]{4,3,2,1,0:T(8,128)S(1)}, f32[2,16,2,8,128]{4,3,2,1,0:T(8,128)S(1)}, u32[]{:S(2)}, u32[]{:S(2)}) collective-permute-start(f32[2,16,2,8,128]{4,3,2,1,0:T(8,128)S(1)} %get-tuple-element.64), channel_id=1, source_target_pairs={{48,0},{96,48},{144,96},{192,144},{240,192},{288,240},{336,288},{3... | collective-permute-start | bytes 786440 | tf_op jit(solution)/shard_map/ppermute | solution.py:19
  216.7 12.7 %collective-permute-start.2 = (f32[2,16,2,8,128]{4,3,2,1,0:T(8,128)S(1)}, f32[2,16,2,8,128]{4,3,2,1,0:T(8,128)S(1)}, u32[]{:S(2)}, u32[]{:S(2)}) collective-permute-start(f32[2,16,2,8,128]{4,3,2,1,0:T(8,128)S(1)} %get-tuple-element.63), channel_id=1, source_target_pairs={{0,48},{48,96},{96,144},{144,192},{192,240},{240,288},{288,336},{3... | collective-permute-start | bytes 786440 | tf_op jit(solution)/shard_map/ppermute | solution.py:17
  221.3 8.2 %copy-start.1 = (f32[1,14,8,128]{3,0,2,1:T(1,128)S(1)}, f32[1,14,8,128]{3,0,2,1:T(1,128)}, u32[]{:S(2)}) copy-start(f32[1,14,8,128]{3,0,2,1:T(1,128)} %get-tuple-element.36) | copy-start | bytes 172036
  221.3 8.2 %copy-start.2 = (f32[1,14,8,128]{3,0,2,1:T(1,128)S(1)}, f32[1,14,8,128]{3,0,2,1:T(1,128)}, u32[]{:S(2)}) copy-start(f32[1,14,8,128]{3,0,2,1:T(1,128)} %get-tuple-element.37) | copy-start | bytes 172036
  221.3 8.2 %copy-start.3 = (f32[1,14,8,128]{3,0,2,1:T(1,128)S(1)}, f32[1,14,8,128]{3,0,2,1:T(1,128)}, u32[]{:S(2)}) copy-start(f32[1,14,8,128]{3,0,2,1:T(1,128)} %get-tuple-element.38) | copy-start | bytes 172036
  221.3 8.2 %copy-start.4 = (f32[1,14,8,128]{3,0,2,1:T(1,128)S(1)}, f32[1,14,8,128]{3,0,2,1:T(1,128)}, u32[]{:S(2)}) copy-start(f32[1,14,8,128]{3,0,2,1:T(1,128)} %get-tuple-element.39) | copy-start | bytes 172036
  221.3 8.2 %copy-start.5 = (f32[1,14,8,128]{3,0,2,1:T(1,128)S(1)}, f32[1,14,8,128]{3,0,2,1:T(1,128)}, u32[]{:S(2)}) copy-start(f32[1,14,8,128]{3,0,2,1:T(1,128)} %get-tuple-element.40) | copy-start | bytes 172036
  221.3 8.2 %copy-start.6 = (f32[1,14,8,128]{3,0,2,1:T(1,128)S(1)}, f32[1,14,8,128]{3,0,2,1:T(1,128)}, u32[]{:S(2)}) copy-start(f32[1,14,8,128]{3,0,2,1:T(1,128)} %get-tuple-element.41) | copy-start | bytes 172036
  221.3 8.2 %copy-start.7 = (f32[1,14,8,128]{3,0,2,1:T(1,128)S(1)}, f32[1,14,8,128]{3,0,2,1:T(1,128)}, u32[]{:S(2)}) copy-start(f32[1,14,8,128]{3,0,2,1:T(1,128)} %get-tuple-element.42) | copy-start | bytes 172036
  221.3 8.2 %copy-start.8 = (f32[1,14,8,128]{3,0,2,1:T(1,128)S(1)}, f32[1,14,8,128]{3,0,2,1:T(1,128)}, u32[]{:S(2)}) copy-start(f32[1,14,8,128]{3,0,2,1:T(1,128)} %get-tuple-element.43) | copy-start | bytes 172036
  221.3 8.2 %copy-start.9 = (f32[1,14,8,128]{3,0,2,1:T(1,128)S(1)}, f32[1,14,8,128]{3,0,2,1:T(1,128)}, u32[]{:S(2)}) copy-start(f32[1,14,8,128]{3,0,2,1:T(1,128)} %get-tuple-element.44) | copy-start | bytes 172036
  221.3 8.2 %copy-start.10 = (f32[1,14,8,128]{3,0,2,1:T(1,128)S(1)}, f32[1,14,8,128]{3,0,2,1:T(1,128)}, u32[]{:S(2)}) copy-start(f32[1,14,8,128]{3,0,2,1:T(1,128)} %get-tuple-element.45) | copy-start | bytes 172036
  221.4 8.2 %copy-start.11 = (f32[1,14,8,128]{3,0,2,1:T(1,128)S(1)}, f32[1,14,8,128]{3,0,2,1:T(1,128)}, u32[]{:S(2)}) copy-start(f32[1,14,8,128]{3,0,2,1:T(1,128)} %get-tuple-element.46) | copy-start | bytes 172036
  221.4 8.2 %copy-start.12 = (f32[1,14,8,128]{3,0,2,1:T(1,128)S(1)}, f32[1,14,8,128]{3,0,2,1:T(1,128)}, u32[]{:S(2)}) copy-start(f32[1,14,8,128]{3,0,2,1:T(1,128)} %get-tuple-element.47) | copy-start | bytes 172036
  221.4 8.2 %copy-start.13 = (f32[1,14,8,128]{3,0,2,1:T(1,128)S(1)}, f32[1,14,8,128]{3,0,2,1:T(1,128)}, u32[]{:S(2)}) copy-start(f32[1,14,8,128]{3,0,2,1:T(1,128)} %get-tuple-element.48) | copy-start | bytes 172036
  221.4 8.2 %copy-start.14 = (f32[1,14,8,128]{3,0,2,1:T(1,128)S(1)}, f32[1,14,8,128]{3,0,2,1:T(1,128)}, u32[]{:S(2)}) copy-start(f32[1,14,8,128]{3,0,2,1:T(1,128)} %get-tuple-element.49) | copy-start | bytes 172036
  221.4 8.2 %copy-start.15 = (f32[1,14,8,128]{3,0,2,1:T(1,128)S(1)}, f32[1,14,8,128]{3,0,2,1:T(1,128)}, u32[]{:S(2)}) copy-start(f32[1,14,8,128]{3,0,2,1:T(1,128)} %get-tuple-element.50) | copy-start | bytes 172036
  221.4 8.2 %copy-start.16 = (f32[1,14,8,128]{3,0,2,1:T(1,128)S(1)}, f32[1,14,8,128]{3,0,2,1:T(1,128)}, u32[]{:S(2)}) copy-start(f32[1,14,8,128]{3,0,2,1:T(1,128)} %get-tuple-element.51) | copy-start | bytes 172036
  221.4 8.2 %copy-start.17 = (f32[1,14,8,128]{3,0,2,1:T(1,128)S(1)}, f32[1,14,8,128]{3,0,2,1:T(1,128)}, u32[]{:S(2)}) copy-start(f32[1,14,8,128]{3,0,2,1:T(1,128)} %get-tuple-element.52) | copy-start | bytes 172036
  229.6 4.8 %copy-start.18 = (f32[1,12,8,128]{3,0,2,1:T(1,128)S(1)}, f32[1,12,8,128]{3,0,2,1:T(1,128)}, u32[]{:S(2)}) copy-start(f32[1,12,8,128]{3,0,2,1:T(1,128)} %get-tuple-element.7) | copy-start | bytes 147460
  229.6 4.8 %copy-start.19 = (f32[1,12,8,128]{3,0,2,1:T(1,128)S(1)}, f32[1,12,8,128]{3,0,2,1:T(1,128)}, u32[]{:S(2)}) copy-start(f32[1,12,8,128]{3,0,2,1:T(1,128)} %get-tuple-element.8) | copy-start | bytes 147460
  229.6 4.8 %copy-start.20 = (f32[1,12,8,128]{3,0,2,1:T(1,128)S(1)}, f32[1,12,8,128]{3,0,2,1:T(1,128)}, u32[]{:S(2)}) copy-start(f32[1,12,8,128]{3,0,2,1:T(1,128)} %get-tuple-element.9) | copy-start | bytes 147460
  238.5 11.5 %collective-permute-start.5 = (f32[2,16,2,8,128]{4,3,2,1,0:T(8,128)S(1)}, f32[2,16,2,8,128]{4,3,2,1,0:T(8,128)S(1)}, u32[]{:S(2)}, u32[]{:S(2)}) collective-permute-start(f32[2,16,2,8,128]{4,3,2,1,0:T(8,128)S(1)} %get-tuple-element.62), channel_id=1, source_target_pairs={{48,0},{96,48},{144,96},{192,144},{240,192},{288,240},{336,288},{3... | collective-permute-start | bytes 786440 | tf_op jit(solution)/shard_map/ppermute | solution.py:19
  243.3 12.7 %collective-permute-start.4 = (f32[2,16,2,8,128]{4,3,2,1,0:T(8,128)S(1)}, f32[2,16,2,8,128]{4,3,2,1,0:T(8,128)S(1)}, u32[]{:S(2)}, u32[]{:S(2)}) collective-permute-start(f32[2,16,2,8,128]{4,3,2,1,0:T(8,128)S(1)} %get-tuple-element.61), channel_id=1, source_target_pairs={{0,48},{48,96},{96,144},{144,192},{192,240},{240,288},{288,336},{3... | collective-permute-start | bytes 786440 | tf_op jit(solution)/shard_map/ppermute | solution.py:17
  (16 other events, 76.7 us)
Sparse Core Ops, SparseCore 0:
  11.4 111.4 all-gather.1
where the time goes:
time: 273 us; the launch traced here: 272 us
  waiting for transfers between devices  160 us (59%)
  local copies, waits for them, and re-layouts  46.6 us (17%)
  starting transfers between devices  27.8 us (10%)
  other arithmetic  18.5 us (7%)
  between operations  14.2 us (5%)
  matrix products  5.49 us (2%)
    all_gather x1, waiting for transfers between devices, local(): columns = lax.all_gather(factor, 'grp', axis=1, tiled=True)  116 us
    scatter x1, local copies, waits for them, and re-layouts, local(): lattice = jnp.zeros_like(moved).at[:, slab_map].set(moved)  33.8 us
    ppermute x3, waiting for transfers between devices, padded_2(): lax.ppermute(head, axis, [((i + 1) % count, i) for i in range(ends)])  27.9 us
    ppermute x3, starting transfers between devices, padded_2(): lax.ppermute(head, axis, [((i + 1) % count, i) for i in range(ends)])  10.9 us
    ppermute x3, waiting for transfers between devices, padded_2(): lax.ppermute(tail, axis, [(i, (i + 1) % count) for i in range(ends)])  10.7 us
    all_to_all x1, starting transfers between devices, local(): lax.all_to_all(rotated, 'grp', split_axis=0, concat_axis=1, tiled=True)  9.29 us
    mul x2, other arithmetic, local(): middle = middle * inside  9.05 us
    ppermute x3, starting transfers between devices, padded_2(): lax.ppermute(tail, axis, [(i, (i + 1) % count) for i in range(ends)])  7.64 us
  transfers between devices with their start and end apart: 8, of which 7 were waited for; matrix products, arithmetic and copies ran while one was open for 2% of the time, Pallas kernels for 0%

commit v1 on v0

v1 whole, which is shorter than its diff:
```python
import functools

import jax
import jax.numpy as jnp
from jax import lax
from jax.experimental import pallas as pl
from jax.experimental.pallas import tpu as pltpu
from jax.sharding import PartitionSpec as P

CHEB = 4
NH = 3
MESH = pl.DeviceIdType.MESH
F32 = jnp.float32
BF16 = jnp.bfloat16


def split(value):
    high = value.astype(BF16)
    low = (value - high.astype(F32)).astype(BF16)
    return high, low


def nt_dot(a, b):
    return lax.dot_general(a, b, (((1,), (1,)), ((), ())), preferred_element_type=F32)


def kernel(
    doms,
    ny,
    feat_ref,
    fac_ref,
    map_ref,
    kinds_ref,
    table_ref,
    out_ref,
    fac_all,
    fcat,
    rot,
    moved,
    acc,
    coef,
    terms,
    z_send,
    z_recv,
    y_send,
    y_recv,
    p_send,
    p_recv,
    a_send,
    a_recv,
    h_send,
    h_recv,
):
    peers = NH * ny * 2
    half = ny // 2
    sb, states = fac_ref.shape
    nb = feat_ref.shape[0]
    kw = states // NH
    planes = kinds_ref.shape[0]
    rows = map_ref.shape[0] * nb // 256

    d = lax.axis_index("dom")
    g = lax.axis_index("grp")
    h = g // (2 * ny)
    y = lax.rem(g // 2, ny)
    c = lax.rem(g, 2)

    def pid(hh, yy, cc):
        return (hh * ny + yy) * 2 + cc

    def wrap(yy):
        return lax.rem(yy + 2 * ny, ny)

    barrier = pltpu.get_barrier_semaphore()

    def greet(i, carry):
        pl.semaphore_signal(barrier, inc=1, device_id=(d, lax.rem(g + i, peers)), device_id_type=MESH)
        return carry

    lax.fori_loop(1, peers, greet, 0)

    @pl.when(d > 0)
    def _():
        pl.semaphore_signal(barrier, inc=1, device_id=(d - 1, g), device_id_type=MESH)

    @pl.when(d < doms - 1)
    def _():
        pl.semaphore_signal(barrier, inc=1, device_id=(d + 1, g), device_id_type=MESH)

    own_rows = pl.ds(pl.multiple_of(g * sb, sb), sb)
    fac_all[own_rows, :] = fac_ref[...]
    f_high, f_low = split(feat_ref[...])
    for t in range(NH):
        part = slice(t * kw, (t + 1) * kw)
        fcat[t, :, 0:kw] = f_high[:, part]
        fcat[t, :, kw : 2 * kw] = f_low[:, part]
        fcat[t, :, 2 * kw : 3 * kw] = f_high[:, part]

    expected = peers - 1 + (d > 0).astype(jnp.int32) + (d < doms - 1).astype(jnp.int32)
    pl.semaphore_wait(barrier, expected)

    def block(hh, yy, cc):
        row = pl.multiple_of(pid(hh, yy, cc) * sb, sb)
        return fac_all.at[pl.ds(row, sb), pl.ds(0, kw * (hh + 1))]

    def z_copy(hs, step):
        to = lax.rem(h + step, NH)
        return pltpu.make_async_remote_copy(
            src_ref=block(hs, y, c),
            dst_ref=block(hs, y, c),
            send_sem=z_send.at[step - 1],
            recv_sem=z_recv.at[hs],
            device_id=(d, pid(to, y, c)),
            device_id_type=MESH,
        )

    def y_copy(slot, hh, from_y, to_y):
        return pltpu.make_async_remote_copy(
            src_ref=block(hh, from_y, c),
            dst_ref=block(hh, from_y, c),
            send_sem=y_send.at[slot, hh],
            recv_sem=y_recv.at[slot, hh],
            device_id=(d, pid(h, to_y, c)),
            device_id_type=MESH,
        )

    def p_copy(slot, hh, yy, cc):
        return pltpu.make_async_remote_copy(
            src_ref=block(hh, yy, cc),
            dst_ref=block(hh, yy, cc),
            send_sem=p_send.at[slot, hh],
            recv_sem=p_recv.at[slot, hh],
            device_id=(d, pid(h, y, 1 - c)),
            device_id_type=MESH,
        )

    right, left = wrap(y + 1), wrap(y - 1)
    last = 2 * half - 1
    last_from = wrap(jnp.where(c == 0, y - (half - 1), y + (half - 1)))
    last_to = jnp.where(c == 0, right, left)

    def slot_y(slot):
        if slot == 0:
            return y
        t = (slot + 1) // 2
        if slot == last:
            return wrap(y + half)
        return wrap(y - t) if slot % 2 == 1 else wrap(y + t)

    for hs in range(NH):

        @pl.when(h == hs)
        def _(hs=hs):
            for step in range(1, NH):
                z_copy(hs, step).start()
            y_copy(1, hs, y, right).start()
            if last != 1:
                y_copy(2, hs, y, left).start()
            p_copy(0, hs, y, c).start()

    for hs in range(NH):

        @pl.when(h != hs)
        def _(hs=hs):
            z_copy(hs, 1).wait_recv()
            y_copy(1, hs, y, right).start()
            if last != 1:
                y_copy(2, hs, y, left).start()
            p_copy(0, hs, y, c).start()

    def a_copy(hh, yy, cc):
        to = pid(hh, yy, cc)
        return pltpu.make_async_remote_copy(
            src_ref=rot.at[to],
            dst_ref=moved.at[g],
            send_sem=a_send.at[to],
            recv_sem=a_recv.at[g],
            device_id=(d, to),
            device_id_type=MESH,
        )

    def rotate(slot):
        yy = slot_y(slot)
        for hh in range(NH):
            p_copy(slot, hh, yy, 1 - c).wait_recv()
        pair = [fac_all[pl.ds(pl.multiple_of(pid(hh, yy, 0) * sb, 2 * sb), 2 * sb), 0 : kw * (hh + 1)] for hh in range(NH)]
        totals = [None] * NH
        for t in range(NH):
            stacked = jnp.concatenate([pair[hh][:, t * kw : (t + 1) * kw] for hh in range(t, NH)], axis=0)
            high, low = split(stacked)
            product = nt_dot(jnp.concatenate([high, high, low], axis=1), fcat[t])
            for hh in range(t, NH):
                piece = product[(hh - t) * 2 * sb : (hh - t + 1) * 2 * sb]
                totals[hh] = piece if totals[hh] is None else totals[hh] + piece
        for hh in range(NH):
            for cc in range(2):
                rot[pid(hh, yy, cc)] = totals[hh][cc * sb : (cc + 1) * sb]
        for step in range(1, NH + 1):
            for cs in range(2):
                hh = lax.rem(h + step, NH)
                cc = lax.rem(c + 1 + cs, 2)
                if slot == 0 and step == NH and cs == 1:
                    moved[g] = rot[g]
                else:
                    a_copy(hh, yy, cc).start()

    rotate(0)
    for t in range(1, half + 1):
        slots = [last] if t == half else [2 * t - 1, 2 * t]
        for hh in range(NH):
            for slot in slots:
                yy = slot_y(slot)
                y_copy(slot, hh, yy, right).wait_recv()
                if t < half - 1:
                    y_copy(slot + 2, hh, yy, right if slot % 2 == 1 else left).start()
                p_copy(slot, hh, yy, c).start()
            if t == half - 1:
                y_copy(last, hh, last_from, last_to).start()
        for slot in slots:
            rotate(slot)

    lane = lax.broadcasted_iota(jnp.int32, kinds_ref.shape[1:], 1)
    sub = lax.broadcasted_iota(jnp.int32, kinds_ref.shape[1:], 0)
    py, pz = kinds_ref.shape[1], kinds_ref.shape[2]

    def coefficients(x, carry):
        for dz in (-1, 0, 1):
            kr = kinds_ref[x]
            if dz != 0:
                kr = pltpu.roll(kr, dz % pz, 1)
            hits = [kr == j for j in range(table_ref.shape[0])]
            for dx in (-1, 0, 1):
                for dy in (-1, 0, 1):
                    o = (dx + 1) * 9 + (dy + 1) * 3 + dz + 1
                    value = jnp.zeros(kr.shape, F32)
                    for j in range(table_ref.shape[0]):
                        value = jnp.where(hits[j], 2.0 * table_ref[j, o], value)
                    if dz == 1:
                        value = jnp.where(lane == 0, 0.0, value)
                    if dz == -1:
                        value = jnp.where(lane == pz - 1, 0.0, value)
                    if dy == 1:
                        value = jnp.where(sub == py - 1, 0.0, value)
                    if dy == -1:
                        value = jnp.where(sub == 0, 0.0, value)
                    coef[x, o] = value
        return carry

    lax.fori_loop(0, planes, coefficients, 0)
    acc[...] = jnp.zeros_like(acc)

    def place(i, carry):
        hh = lax.rem(i, NH)
        slot = i // NH
        t = (slot + 1) // 2
        yy = wrap(jnp.where(lax.rem(slot, 2) == 1, y + t, y - t))
        a_parts, b_parts = [], []
        for cc in range(2):
            src = pid(hh, yy, cc)

            @pl.when(src != g)
            def _(src=src):
                pltpu.make_async_remote_copy(
                    src_ref=rot.at[src],
                    dst_ref=moved.at[src],
                    send_sem=a_send.at[src],
                    recv_sem=a_recv.at[src],
                    device_id=(d, src),
                    device_id_type=MESH,
                ).wait_recv()

            cell = map_ref[pl.ds(src, 1), :]
            row = (cell // 2048) * 8 + lax.rem(cell // 128, 8)
            column = lax.rem(cell // 1024, 2) * 128 + lax.rem(cell, 128)
            high, low = split(moved[src])
            row16 = jnp.broadcast_to(row.astype(F32), (sb, nb)).astype(BF16)
            for value in (high, low):
                a_parts.append(
                    jnp.concatenate([jnp.where(row16 == BF16(r), value, BF16(0)) for r in range(rows)], axis=0)
                )
            wide = jnp.broadcast_to(column, (256, nb))
            onehot = (wide == lax.broadcasted_iota(jnp.int32, (256, nb), 0)).astype(F32).astype(BF16)
            b_parts += [onehot, onehot]
        product = nt_dot(jnp.concatenate(a_parts, axis=1), jnp.concatenate(b_parts, axis=1))
        acc[0] += product[:, 0:128]
        acc[1] += product[:, 128:256]
        return carry

    lax.fori_loop(0, NH * ny, place, 0)

    def lift(x):
        def one(s, carry):
            terms[0, x + 1, s] = acc[x % 2 if isinstance(x, int) else 0, pl.ds((x // 2) * 8 * sb + s, 8, stride=sb), :]
            return carry

        lax.fori_loop(0, sb, one, 0, unroll=4)

    def halo(k, up):
        to = d + 1 if up else d - 1
        return pltpu.make_async_remote_copy(
            src_ref=terms.at[k, planes if up else 1],
            dst_ref=terms.at[k, 0 if up else planes + 1],
            send_sem=h_send.at[k, 0 if up else 1],
            recv_sem=h_recv.at[k, 0 if up else 1],
            device_id=(to, g),
            device_id_type=MESH,
        )

    def send_edges(k):
        @pl.when(d < doms - 1)
        def _():
            halo(k, True).start()

        @pl.when(d > 0)
        def _():
            halo(k, False).start()

    def wait_edges(k):
        @pl.when(d > 0)
        def _():
            halo(k, True).wait_recv()

        @pl.when(d < doms - 1)
        def _():
            halo(k, False).wait_recv()

    @pl.when(d == 0)
    def _():
        for k in range(CHEB):
            terms[k, 0] = jnp.zeros(terms.shape[2:], F32)

    @pl.when(d == doms - 1)
    def _():
        for k in range(CHEB):
            terms[k, planes + 1] = jnp.zeros(terms.shape[2:], F32)

    lift(0)
    lift(planes - 1)
    send_edges(0)
    for x in range(1, planes - 1):
        lift(x)

    def plane(k, x):
        cs = [coef[x, o] for o in range(27)]

        def one(s, carry):
            sums = [None, None, None]
            for dx in range(3):
                mid = terms[k, x + dx, s]
                shifted = (pltpu.roll(mid, 1, 0), mid, pltpu.roll(mid, py - 1, 0))
                for dy in range(3):
                    for dz in range(3):
                        term = cs[dx * 9 + dy * 3 + dz] * shifted[dy]
                        sums[dz] = term if sums[dz] is None else sums[dz] + term
            total = sums[1] + pltpu.roll(sums[0], 1, 1) + pltpu.roll(sums[2], pz - 1, 1)
            if k == 0:
                total = 0.5 * total
            else:
                total = total - terms[k - 1, x + 1, s]
            if k == CHEB - 1:
                out_ref[s, x] = total
            else:
                terms[k + 1, x + 1, s] = total
            return carry

        lax.fori_loop(0, sb, one, 0, unroll=4)

    for k in range(CHEB):

        def interior(x, carry, k=k):
            plane(k, x)
            return carry

        lax.fori_loop(1, planes - 1, interior, 0)
        wait_edges(k)
        plane(k, 0)
        plane(k, planes - 1)
        if k < CHEB - 1:
            send_edges(k + 1)

    for step in range(1, NH):
        for hs in range(NH):

            @pl.when(h == hs)
            def _(hs=hs, step=step):
                z_copy(hs, step).wait_send()

    for slot in range(1, 2 * half):
        for hh in range(NH):
            y_copy(slot, hh, y, right).wait_send()
    for slot in range(2 * half):
        for hh in range(NH):
            p_copy(slot, hh, y, c).wait_send()

    def sent(i, carry):
        to = lax.rem(g + i, peers)
        pltpu.make_async_remote_copy(
            src_ref=rot.at[to],
            dst_ref=moved.at[g],
            send_sem=a_send.at[to],
            recv_sem=a_recv.at[g],
            device_id=(d, to),
            device_id_type=MESH,
        ).wait_send()
        return carry

    lax.fori_loop(1, peers, sent, 0)
    for k in range(CHEB):

        @pl.when(d < doms - 1)
        def _(k=k):
            halo(k, True).wait_send()

        @pl.when(d > 0)
        def _(k=k):
            halo(k, False).wait_send()


def local(doms, peers, features, factor, slab_map, kinds, kind_table):
    nb, states = features.shape
    sb = factor.shape[1]
    ny = peers // (2 * NH)
    planes, py, pz = kinds.shape
    cells = slab_map.shape[0]
    dma = pltpu.SemaphoreType.DMA
    vmem = pl.BlockSpec(memory_space=pltpu.VMEM)
    return pl.pallas_call(
        functools.partial(kernel, doms, ny),
        out_shape=jax.ShapeDtypeStruct((sb, planes, py, pz), F32),
        in_specs=[vmem, vmem, vmem, vmem, pl.BlockSpec(memory_space=pltpu.SMEM)],
        out_specs=vmem,
        scratch_shapes=[
            pltpu.VMEM((states, states), F32),
            pltpu.VMEM((NH, nb, states), BF16),
            pltpu.VMEM((peers, sb, nb), F32),
            pltpu.VMEM((peers, sb, nb), F32),
            pltpu.VMEM((2, cells // 256 * sb, 128), F32),
            pltpu.VMEM((planes, 27, py, pz), F32),
            pltpu.VMEM((CHEB, planes + 2, sb, py, pz), F32),
            dma((NH - 1,)),
            dma((NH,)),
            dma((ny, NH)),
            dma((ny, NH)),
            dma((ny, NH)),
            dma((ny, NH)),
            dma((peers,)),
            dma((peers,)),
            dma((CHEB, 2)),
            dma((CHEB, 2)),
        ],
        compiler_params=pltpu.CompilerParams(
            collective_id=0, has_side_effects=True, vmem_limit_bytes=48 * 1024 * 1024
        ),
    )(features, factor.T, slab_map.reshape(peers, nb), kinds, kind_table)


def solution(mesh):
    return jax.shard_map(
        functools.partial(local, mesh.shape["dom"], mesh.shape["grp"]),
        mesh=mesh,
        in_specs=(P(("dom", "grp"), None), P(None, "grp"), P("dom"), P("dom", None, None), P()),
        out_specs=P("grp", "dom", None, None),
        check_vma=False,
    )
```

time: 273 us -> 103 us (0.38)
  waiting for transfers between devices: 160 us -> 0 us
  Pallas kernels: 0 us -> 98.7 us
  local copies, waits for them, and re-layouts: 46.6 us -> 3.53 us
  starting transfers between devices: 27.8 us -> 0 us
  other arithmetic: 18.5 us -> 0 us
  between operations: 14.2 us -> 0.03 us
  matrix products: 5.49 us -> 0 us
    all_gather x1 -> x0, waiting for transfers between devices: 116 us -> none  [local(): columns = lax.all_gather(factor, 'grp', axis=1, tiled=True)]
    pallas_call x0 -> x1, Pallas kernels: none -> 98.7 us  [local(): pl.pallas_call(functools.partial(kernel, doms, ny), out_shape=jax.ShapeDt...]
    ppermute x6 -> x0, waiting for transfers between devices: 38.6 us -> none  [the longest x3 27.9 us: padded_2(): lax.ppermute(head, axis, [((i + 1) % count, i) for i in range(ends)])]
    scatter x1 -> x0, local copies, waits for them, and re-layouts: 33.8 us -> none  [local(): lattice = jnp.zeros_like(moved).at[:, slab_map].set(moved)]
    ppermute x6 -> x0, starting transfers between devices: 18.5 us -> none  [the longest x3 10.9 us: padded_2(): lax.ppermute(head, axis, [((i + 1) % count, i) for i in range(ends)])]
    all_to_all x1 -> x0, starting transfers between devices: 9.29 us -> none  [local(): lax.all_to_all(rotated, 'grp', split_axis=0, concat_axis=1, tiled=True)]
    mul x2 -> x0, other arithmetic: 9.05 us -> none  [local(): middle = middle * inside]
    dot_general x2 -> x0, matrix products: 5.49 us -> none  [the longest x1 4.57 us: local(): lax.dot_general(columns, features, numbers, precision=lax.Precision.HIGHE...]
  transfers between devices with their start and end apart: 8 -> 0, of which waited for: 7 -> 0; matrix products, arithmetic and copies ran while one was open for 2% -> 0% of each run, Pallas kernels for 0% -> 0%
where the time goes in v1:
time: 103 us; the launch traced here: 102 us
  Pallas kernels  98.7 us (96%)
  local copies, waits for them, and re-layouts  3.53 us (3%)
    pallas_call x1, Pallas kernels, local(): pl.pallas_call(functools.partial(kernel, doms, ny), out_shape=jax.ShapeDt...  98.7 us
    unnamed x9, local copies, waits for them, and re-layouts  2.71 us

profile of v1, /device:TPU:6, one launch (start us, length us, event | category | flops | bytes accessed | tf_op | source)
XLA Modules:
  0.0 102.3 jit_solution(8907001163424255839)
XLA Ops:
  0.0 0.0 copy-start.1
  0.0 0.0 copy-start.2
  0.0 0.8 reshape.3.map_ref
  0.8 0.0 copy-done.1
  0.8 0.0 copy-done.2
  0.8 0.0 copy-start
  0.9 1.1 %copy-done = f32[256,768]{1,0:T(8,128)S(1)} copy-done((f32[256,768]{1,0:T(8,128)S(1)}, f32[256,768]{1,0:T(8,128)}, u32[]{:S(2)}) %copy-start) | copy-done | bytes 786456
  2.0 0.0 copy-start.3
  2.0 0.7 copy-done.3
  2.7 98.7 %shard_map.55 = f32[16,12,8,128]{3,2,1,0:T(8,128)S(1)} custom-call(f32[256,768]{1,0:T(8,128)S(1)} %copy-done, f32[16,768]{1,0:T(8,128)S(1)} %bitcast.1, s32[48,256]{1,0:T(8,128)S(1)} %reshape.3.map_ref, s32[12,8,128]{2,1,0:T(8,128)S(1)} %copy-done.2, f32[8,27]{1,0:T(8,128)S(1)} %copy-done.3), custom_call_target="tpu_custom_call" | custom-call | tf_op jit(solution)/shard_map/pallas_call | solution.py:427
  101.4 0.9 copy.7
Async XLA Ops:
  0.0 0.8 copy-start.1
  0.0 0.8 copy-start.2
  0.8 1.1 %copy-start = (f32[256,768]{1,0:T(8,128)S(1)}, f32[256,768]{1,0:T(8,128)}, u32[]{:S(2)}) copy-start(f32[256,768]{1,0:T(8,128)} %feat_ref.1) | copy-start | bytes 2359300
  2.0 0.7 copy-start.3

commit v2 on v1

--- a/solution.py
+++ b/solution.py
@@ -9,6 +9,8 @@
 
 CHEB = 4
 NH = 3
+DEEP = CHEB - 1
+LAG = 2
 MESH = pl.DeviceIdType.MESH
 F32 = jnp.float32
 BF16 = jnp.bfloat16
@@ -27,12 +29,15 @@
 def kernel(
     doms,
     ny,
+    feat_hbm,
+    fac_hbm,
+    map_hbm,
+    kinds_hbm,
+    table_ref,
+    out_ref,
     feat_ref,
-    fac_ref,
     map_ref,
     kinds_ref,
-    table_ref,
-    out_ref,
     fac_all,
     fcat,
     rot,
@@ -50,14 +55,17 @@
     a_recv,
     h_send,
     h_recv,
+    k_send,
+    k_recv,
+    fetched,
 ):
     peers = NH * ny * 2
     half = ny // 2
-    sb, states = fac_ref.shape
-    nb = feat_ref.shape[0]
+    sb, states = fac_hbm.shape
+    nb = feat_hbm.shape[0]
     kw = states // NH
-    planes = kinds_ref.shape[0]
-    rows = map_ref.shape[0] * nb // 256
+    planes = kinds_hbm.shape[0]
+    rows = map_hbm.shape[0] * map_hbm.shape[1] // 256
 
     d = lax.axis_index("dom")
     g = lax.axis_index("grp")
@@ -71,13 +79,21 @@
     def wrap(yy):
         return lax.rem(yy + 2 * ny, ny)
 
+    own_rows = pl.ds(pl.multiple_of(g * sb, sb), sb)
+    fetches = [
+        pltpu.make_async_copy(fac_hbm, fac_all.at[own_rows], fetched.at[0]),
+        pltpu.make_async_copy(feat_hbm, feat_ref, fetched.at[1]),
+        pltpu.make_async_copy(kinds_hbm, kinds_ref.at[pl.ds(DEEP, planes)], fetched.at[2]),
+        pltpu.make_async_copy(map_hbm, map_ref, fetched.at[3]),
+    ]
+    for fetch in fetches:
+        fetch.start()
+
     barrier = pltpu.get_barrier_semaphore()
-
-    def greet(i, carry):
-        pl.semaphore_signal(barrier, inc=1, device_id=(d, lax.rem(g + i, peers)), device_id_type=MESH)
-        return carry
-
-    lax.fori_loop(1, peers, greet, 0)
+    near = [pid(h, wrap(y + 1), c), pid(h, wrap(y - 1), c), pid(h, y, 1 - c)]
+    near += [pid(lax.rem(h + step, NH), y, c) for step in range(1, NH)]
+    for to in near:
+        pl.semaphore_signal(barrier, inc=1, device_id=(d, to), device_id_type=MESH)
 
     @pl.when(d > 0)
     def _():
@@ -87,8 +103,8 @@
     def _():
         pl.semaphore_signal(barrier, inc=1, device_id=(d + 1, g), device_id_type=MESH)
 
-    own_rows = pl.ds(pl.multiple_of(g * sb, sb), sb)
-    fac_all[own_rows, :] = fac_ref[...]
+    for fetch in fetches:
+        fetch.wait()
     f_high, f_low = split(feat_ref[...])
     for t in range(NH):
         part = slice(t * kw, (t + 1) * kw)
@@ -96,7 +112,7 @@
         fcat[t, :, kw : 2 * kw] = f_low[:, part]
         fcat[t, :, 2 * kw : 3 * kw] = f_high[:, part]
 
-    expected = peers - 1 + (d > 0).astype(jnp.int32) + (d < doms - 1).astype(jnp.int32)
+    expected = len(near) + (d > 0).astype(jnp.int32) + (d < doms - 1).astype(jnp.int32)
     pl.semaphore_wait(barrier, expected)
 
     def block(hh, yy, cc):
@@ -204,28 +220,36 @@
                 else:
                     a_copy(hh, yy, cc).start()
 
-    rotate(0)
-    for t in range(1, half + 1):
-        slots = [last] if t == half else [2 * t - 1, 2 * t]
-        for hh in range(NH):
-            for slot in slots:
-                yy = slot_y(slot)
-                y_copy(slot, hh, yy, right).wait_recv()
-                if t < half - 1:
-                    y_copy(slot + 2, hh, yy, right if slot % 2 == 1 else left).start()
-                p_copy(slot, hh, yy, c).start()
-            if t == half - 1:
-                y_copy(last, hh, last_from, last_to).start()
-        for slot in slots:
-            rotate(slot)
-
-    lane = lax.broadcasted_iota(jnp.int32, kinds_ref.shape[1:], 1)
-    sub = lax.broadcasted_iota(jnp.int32, kinds_ref.shape[1:], 0)
-    py, pz = kinds_ref.shape[1], kinds_ref.shape[2]
-
-    def coefficients(x, carry):
+    lane = lax.broadcasted_iota(jnp.int32, kinds_hbm.shape[1:], 1)
+    sub = lax.broadcasted_iota(jnp.int32, kinds_hbm.shape[1:], 0)
+    py, pz = kinds_hbm.shape[1], kinds_hbm.shape[2]
+
+    first_in = jnp.where(d == 0, DEEP, 0)
+    first_out = jnp.where(d == doms - 1, planes + DEEP, planes + 2 * DEEP)
+
+    def k_copy(up):
+        size = pl.ds(planes if up else DEEP, DEEP)
+        return pltpu.make_async_remote_copy(
+            src_ref=kinds_ref.at[size],
+            dst_ref=kinds_ref.at[pl.ds(0 if up else planes + DEEP, DEEP)],
+            send_sem=k_send.at[0 if up else 1],
+            recv_sem=k_recv.at[0 if up else 1],
+            device_id=(d + 1 if up else d - 1, g),
+            device_id_type=MESH,
+        )
+
+    @pl.when(d < doms - 1)
+    def _():
+        k_copy(True).start()
+
+    @pl.when(d > 0)
+    def _():
+        k_copy(False).start()
+
+    def coefficients(i, carry):
+        inside = jnp.logical_and(i >= first_in, i < first_out)
         for dz in (-1, 0, 1):
-            kr = kinds_ref[x]
+            kr = kinds_ref[i]
             if dz != 0:
                 kr = pltpu.roll(kr, dz % pz, 1)
             hits = [kr == j for j in range(table_ref.shape[0])]
@@ -243,11 +267,27 @@
                         value = jnp.where(sub == py - 1, 0.0, value)
                     if dy == -1:
                         value = jnp.where(sub == 0, 0.0, value)
-                    coef[x, o] = value
+                    coef[i, o] = jnp.where(inside, value, 0.0)
         return carry
 
-    lax.fori_loop(0, planes, coefficients, 0)
-    acc[...] = jnp.zeros_like(acc)
+    def make_coefficients():
+        @pl.when(d == 0)
+        def _():
+            kinds_ref[0:DEEP] = jnp.zeros((DEEP, py, pz), jnp.int32)
+
+        @pl.when(d == doms - 1)
+        def _():
+            kinds_ref[planes + DEEP : planes + 2 * DEEP] = jnp.zeros((DEEP, py, pz), jnp.int32)
+
+        @pl.when(d > 0)
+        def _():
+            k_copy(True).wait_recv()
+
+        @pl.when(d < doms - 1)
+        def _():
+            k_copy(False).wait_recv()
+
+        lax.fori_loop(0, planes + 2 * DEEP, coefficients, 0)
 
     def place(i, carry):
         hh = lax.rem(i, NH)
@@ -269,7 +309,7 @@
                     device_id_type=MESH,
                 ).wait_recv()
 
-            cell = map_ref[pl.ds(src, 1), :]
+            cell = jnp.concatenate([map_ref[pl.ds(2 * src + i, 1), :] for i in range(2)], axis=1)
             row = (cell // 2048) * 8 + lax.rem(cell // 128, 8)
             column = lax.rem(cell // 1024, 2) * 128 + lax.rem(cell, 128)
             high, low = split(moved[src])
@@ -286,84 +326,93 @@
         acc[1] += product[:, 128:256]
         return carry
 
-    lax.fori_loop(0, NH * ny, place, 0)
+    rotate(0)
+    make_coefficients()
+    acc[...] = jnp.zeros_like(acc)
+    placed = 0
+    for t in range(1, half + 1):
+        slots = [last] if t == half else [2 * t - 1, 2 * t]
+        for hh in range(NH):
+            for slot in slots:
+                yy = slot_y(slot)
+                y_copy(slot, hh, yy, right).wait_recv()
+                if t < half - 1:
+                    y_copy(slot + 2, hh, yy, right if slot % 2 == 1 else left).start()
+                p_copy(slot, hh, yy, c).start()
+            if t == half - 1:
+                y_copy(last, hh, last_from, last_to).start()
+        for slot in slots:
+            rotate(slot)
+        ready = max(2 * (t - LAG) + 1, 0)
+        if ready > placed:
+            lax.fori_loop(placed * NH, ready * NH, place, 0)
+            placed = ready
+    lax.fori_loop(placed * NH, ny * NH, place, 0)
 
     def lift(x):
         def one(s, carry):
-            terms[0, x + 1, s] = acc[x % 2 if isinstance(x, int) else 0, pl.ds((x // 2) * 8 * sb + s, 8, stride=sb), :]
+            terms[0, x + CHEB, s] = acc[x % 2, pl.ds((x // 2) * py * sb + s, py, stride=sb), :]
             return carry
 
-        lax.fori_loop(0, sb, one, 0, unroll=4)
-
-    def halo(k, up):
-        to = d + 1 if up else d - 1
+        lax.fori_loop(0, sb, one, 0, unroll=True)
+
+    def halo(j, up):
         return pltpu.make_async_remote_copy(
-            src_ref=terms.at[k, planes if up else 1],
-            dst_ref=terms.at[k, 0 if up else planes + 1],
-            send_sem=h_send.at[k, 0 if up else 1],
-            recv_sem=h_recv.at[k, 0 if up else 1],
-            device_id=(to, g),
+            src_ref=terms.at[0, CHEB + planes - j if up else CHEB + j - 1],
+            dst_ref=terms.at[0, CHEB - j if up else CHEB + planes + j - 1],
+            send_sem=h_send.at[j - 1, 0 if up else 1],
+            recv_sem=h_recv.at[j - 1, 0 if up else 1],
+            device_id=(d + 1 if up else d - 1, g),
             device_id_type=MESH,
         )
 
-    def send_edges(k):
+    @pl.when(d == 0)
+    def _():
+        terms[0, 0:CHEB] = jnp.zeros((CHEB,) + terms.shape[2:], F32)
+
+    @pl.when(d == doms - 1)
+    def _():
+        terms[0, planes + CHEB : planes + 2 * CHEB] = jnp.zeros((CHEB,) + terms.shape[2:], F32)
+
+    lifted = []
+    for j in range(1, CHEB + 1):
+        for x in (planes - j, j - 1):
+            if x not in lifted:
+                lift(x)
+                lifted.append(x)
+
         @pl.when(d < doms - 1)
-        def _():
-            halo(k, True).start()
+        def _(j=j):
+            halo(j, True).start()
 
         @pl.when(d > 0)
-        def _():
-            halo(k, False).start()
-
-    def wait_edges(k):
-        @pl.when(d > 0)
-        def _():
-            halo(k, True).wait_recv()
-
-        @pl.when(d < doms - 1)
-        def _():
-            halo(k, False).wait_recv()
-
-    @pl.when(d == 0)
-    def _():
-        for k in range(CHEB):
-            terms[k, 0] = jnp.zeros(terms.shape[2:], F32)
-
-    @pl.when(d == doms - 1)
-    def _():
-        for k in range(CHEB):
-            terms[k, planes + 1] = jnp.zeros(terms.shape[2:], F32)
-
-    lift(0)
-    lift(planes - 1)
-    send_edges(0)
-    for x in range(1, planes - 1):
-        lift(x)
+        def _(j=j):
+            halo(j, False).start()
+
+    for x in range(planes):
+        if x not in lifted:
+            lift(x)
 
     def plane(k, x):
-        cs = [coef[x, o] for o in range(27)]
-
-        def one(s, carry):
+        for first in range(0, sb, 4):
+            block = slice(first, first + 4)
             sums = [None, None, None]
             for dx in range(3):
-                mid = terms[k, x + dx, s]
-                shifted = (pltpu.roll(mid, 1, 0), mid, pltpu.roll(mid, py - 1, 0))
+                mid = terms[k, x + CHEB - 1 + dx, block]
+                shifted = (pltpu.roll(mid, 1, 1), mid, pltpu.roll(mid, py - 1, 1))
                 for dy in range(3):
                     for dz in range(3):
-                        term = cs[dx * 9 + dy * 3 + dz] * shifted[dy]
+                        term = coef[x + DEEP, dx * 9 + dy * 3 + dz][None] * shifted[dy]
                         sums[dz] = term if sums[dz] is None else sums[dz] + term
-            total = sums[1] + pltpu.roll(sums[0], 1, 1) + pltpu.roll(sums[2], pz - 1, 1)
+            total = sums[1] + pltpu.roll(sums[0], 1, 2) + pltpu.roll(sums[2], pz - 1, 2)
             if k == 0:
                 total = 0.5 * total
             else:
-                total = total - terms[k - 1, x + 1, s]
+                total = total - terms[k - 1, x + CHEB, block]
             if k == CHEB - 1:
-                out_ref[s, x] = total
+                out_ref[block, x] = total
             else:
-                terms[k + 1, x + 1, s] = total
-            return carry
-
-        lax.fori_loop(0, sb, one, 0, unroll=4)
+                terms[k + 1, x + CHEB, block] = total
 
     for k in range(CHEB):
 
@@ -371,12 +420,25 @@
             plane(k, x)
             return carry
 
-        lax.fori_loop(1, planes - 1, interior, 0)
-        wait_edges(k)
-        plane(k, 0)
-        plane(k, planes - 1)
-        if k < CHEB - 1:
-            send_edges(k + 1)
+        lax.fori_loop(k + 1, planes - 1 - k, interior, 0)
+    for j in range(1, CHEB + 1):
+
+        @pl.when(d > 0)
+        def _(j=j):
+            halo(j, True).wait_recv()
+
+        @pl.when(d < doms - 1)
+        def _(j=j):
+            halo(j, False).wait_recv()
+
+        for k in range(CHEB):
+            low, high = k + 1 - j, planes - 2 - k + j
+
+            def both(i, carry, k=k, low=low, high=high):
+                plane(k, low + i * (high - low))
+                return carry
+
+            lax.fori_loop(0, 2, both, 0)
 
     for step in range(1, NH):
         for hs in range(NH):
@@ -405,15 +467,17 @@
         return carry
 
     lax.fori_loop(1, peers, sent, 0)
-    for k in range(CHEB):
-
-        @pl.when(d < doms - 1)
-        def _(k=k):
-            halo(k, True).wait_send()
-
-        @pl.when(d > 0)
-        def _(k=k):
-            halo(k, False).wait_send()
+    @pl.when(d < doms - 1)
+    def _():
+        k_copy(True).wait_send()
+        for j in range(1, CHEB + 1):
+            halo(j, True).wait_send()
+
+    @pl.when(d > 0)
+    def _():
+        k_copy(False).wait_send()
+        for j in range(1, CHEB + 1):
+            halo(j, False).wait_send()
 
 
 def local(doms, peers, features, factor, slab_map, kinds, kind_table):
@@ -427,16 +491,19 @@
     return pl.pallas_call(
         functools.partial(kernel, doms, ny),
         out_shape=jax.ShapeDtypeStruct((sb, planes, py, pz), F32),
-        in_specs=[vmem, vmem, vmem, vmem, pl.BlockSpec(memory_space=pltpu.SMEM)],
+        in_specs=[pl.BlockSpec(memory_space=pltpu.HBM)] * 4 + [pl.BlockSpec(memory_space=pltpu.SMEM)],
         out_specs=vmem,
         scratch_shapes=[
+            pltpu.VMEM((nb, states), F32),
+            pltpu.VMEM((cells // 128, 128), jnp.int32),
+            pltpu.VMEM((planes + 2 * DEEP, py, pz), jnp.int32),
             pltpu.VMEM((states, states), F32),
             pltpu.VMEM((NH, nb, states), BF16),
             pltpu.VMEM((peers, sb, nb), F32),
             pltpu.VMEM((peers, sb, nb), F32),
             pltpu.VMEM((2, cells // 256 * sb, 128), F32),
-            pltpu.VMEM((planes, 27, py, pz), F32),
-            pltpu.VMEM((CHEB, planes + 2, sb, py, pz), F32),
+            pltpu.VMEM((planes + 2 * DEEP, 27, py, pz), F32),
+            pltpu.VMEM((CHEB, planes + 2 * CHEB, sb, py, pz), F32),
             dma((NH - 1,)),
             dma((NH,)),
             dma((ny, NH)),
@@ -447,11 +514,14 @@
             dma((peers,)),
             dma((CHEB, 2)),
             dma((CHEB, 2)),
+            dma((2,)),
+            dma((2,)),
+            dma((4,)),
         ],
         compiler_params=pltpu.CompilerParams(
-            collective_id=0, has_side_effects=True, vmem_limit_bytes=48 * 1024 * 1024
+            collective_id=0, has_side_effects=True, vmem_limit_bytes=63 * 1024 * 1024
         ),
-    )(features, factor.T, slab_map.reshape(peers, nb), kinds, kind_table)
+    )(features, factor.T, slab_map.reshape(cells // 128, 128), kinds, kind_table)
 
 
 def solution(mesh):

time: 103 us -> 84.1 us (0.82)
  the two profiles are of different devices: /device:TPU:6 before, /device:TPU:3 now
where the time goes in v2:
time: 84.1 us; the launch traced here: 83.8 us
  Pallas kernels  81.8 us (97%)
  local copies, waits for them, and re-layouts  2.07 us (2%)
    pallas_call x1, Pallas kernels, local(): pl.pallas_call(functools.partial(kernel, doms, ny), out_shape=jax.ShapeDt...  81.8 us
    unnamed x1, local copies, waits for them, and re-layouts  2.07 us

profile of v2, /device:TPU:3, one launch (start us, length us, event | category | flops | bytes accessed | tf_op | source)
XLA Modules:
  0.0 83.8 jit_solution(8885839869965285020)
XLA Ops:
  0.0 81.8 %shard_map.55 = f32[16,12,8,128]{3,2,1,0:T(8,128)} custom-call(f32[256,768]{1,0:T(8,128)} %feat_hbm.1, f32[16,768]{1,0:T(8,128)} %bitcast.2, s32[96,128]{1,0:T(8,128)} %bitcast.3, s32[12,8,128]{2,1,0:T(8,128)} %kinds_hbm.1, f32[8,27]{1,0:T(8,128)} %table_ref.1), custom_call_target="tpu_custom_call" | custom-call | tf_op jit(solution)/shard_map/pallas_call | solution.py:491
  81.8 2.1 %copy.7 = f32[16,12,8,128]{3,2,1,0:T(8,128)} copy(f32[16,12,8,128]{3,2,1,0:T(8,128)} %shard_map.55) | data formatting | bytes 1572864

commit v3 on v2

--- a/solution.py
+++ b/solution.py
@@ -10,7 +10,7 @@
 CHEB = 4
 NH = 3
 DEEP = CHEB - 1
-LAG = 2
+LAG = 1
 MESH = pl.DeviceIdType.MESH
 F32 = jnp.float32
 BF16 = jnp.bfloat16

time: 84.1 us -> 89.9 us (1.069)
  the two profiles are of different devices: /device:TPU:3 before, /device:TPU:68 now
where the time goes in v3:
time: 89.9 us; the launch traced here: 89.7 us
  Pallas kernels  87.6 us (97%)
  local copies, waits for them, and re-layouts  2.07 us (2%)
    pallas_call x1, Pallas kernels, local(): pl.pallas_call(functools.partial(kernel, doms, ny), out_shape=jax.ShapeDt...  87.6 us
    unnamed x1, local copies, waits for them, and re-layouts  2.07 us

profile of v3, /device:TPU:68, one launch (start us, length us, event | category | flops | bytes accessed | tf_op | source)
XLA Modules:
  0.0 89.7 jit_solution(15061362403193875894)
XLA Ops:
  0.0 87.6 %shard_map.55 = f32[16,12,8,128]{3,2,1,0:T(8,128)} custom-call(f32[256,768]{1,0:T(8,128)} %feat_hbm.1, f32[16,768]{1,0:T(8,128)} %bitcast.2, s32[96,128]{1,0:T(8,128)} %bitcast.3, s32[12,8,128]{2,1,0:T(8,128)} %kinds_hbm.1, f32[8,27]{1,0:T(8,128)} %table_ref.1), custom_call_target="tpu_custom_call" | custom-call | tf_op jit(solution)/shard_map/pallas_call | solution.py:491
  87.7 2.1 %copy.7 = f32[16,12,8,128]{3,2,1,0:T(8,128)} copy(f32[16,12,8,128]{3,2,1,0:T(8,128)} %shard_map.55) | data formatting | bytes 1572864
